TPU v7x, 32 devices: a whole 2x2x4 slice. The times are simulated.
32 devices in a mesh: group: 2 (over y), stn: 8 (over z, x), chan: 2 (over core).
Axes of the slice: x: 2, y: 2, z: 4, core: 2. Of those that a mesh axis runs over, the one named last changes fastest.
Arguments:
- gradient: float32 [65536], P(('group', 'stn')), parts along dimension 0, may hold values from -24 to 24
- normal_blocks: bfloat16 [2, 512, 5, 128, 128], P('chan', ('group', 'stn')), parts along dimension 1, may hold values from -0.2 to 4.2
- pattern: int32 [512, 5], P(('group', 'stn')), parts along dimension 0, may hold values from 0 to 255, as said below
Outputs:
- solution: float32 [65536], P(('group', 'stn')), parts along dimension 0
- residual: float32 [65536], P(('group', 'stn')), parts along dimension 0
There are 2 independent parts, one for each index of `group`. A program takes and returns all parts, laid end to end along the dimension named above; each array names one. Nothing has to cross between parts.
Inputs may be any that keep to these rules, and one draw needn't show every extreme that they name: pattern[n, 0] = n. Block rows come in station groups of 32 (group n // 32); tile 3 lies in the group exactly 4 away from that of n; every other column block of row n lies in a group whose number differs from that of n by at most 3 modulo 8, tile 1 exactly 3 groups ahead and tile 2 exactly 3 behind.
All inputs are finite; a program needn't handle non-finite values.
Results may differ from a plain program's by a relative error of at most 0.011.
Values may be sent and summed in bfloat16 or wider, within the bound.
A program may use at most 64 MiB of HBM per device.

v0:
```python
import jax
import jax.numpy as jnp
from jax import lax
from jax.sharding import PartitionSpec as P

ITERS = 2


def local(gradient, normal_blocks, pattern):
    blocks = normal_blocks[0]
    block_rows = blocks.shape[0]
    width = blocks.shape[2]
    solution = jnp.zeros_like(gradient)
    residual = gradient
    direction = gradient
    norm_now = lax.psum(jnp.sum(residual * residual), "stn")
    for step in range(ITERS):
        rounded = direction.astype(jnp.bfloat16).reshape(block_rows, width)
        whole = lax.all_gather(rounded, "stn", axis=0, tiled=True)
        picked = whole[pattern]
        partial_value = jnp.einsum(
            "nkij,nkj->ni", blocks, picked, preferred_element_type=jnp.float32
        )
        image = lax.psum(partial_value.reshape(-1), "chan")
        curve = lax.psum(jnp.sum(direction * image), "stn")
        alpha = norm_now / curve
        solution = solution + alpha * direction
        residual = residual - alpha * image
        norm_next = lax.psum(jnp.sum(residual * residual), "stn")
        direction = residual + norm_next / norm_now * direction
        norm_now = norm_next
    return (solution, residual)


def solution(mesh):
    placed = (
        P(("group", "stn")),
        P("chan", ("group", "stn"), None, None, None),
        P(("group", "stn"), None),
    )
    return jax.shard_map(
        local,
        mesh=mesh,
        in_specs=placed,
        out_specs=(P(("group", "stn")), P(("group", "stn"))),
        check_vma=False,
    )
```

profile of v0, /device:TPU:0, one launch (start us, length us, event | category | flops | bytes accessed | tf_op | source)
XLA Modules:
  0.0 147.7 jit_solution(8259339369132344353)
XLA Ops:
  0.6 0.0 copy-start
  0.6 0.7 compare_select_fusion
  1.3 0.7 convert_bitcast_fusion.1
  2.1 0.1 copy.5
  2.1 0.1 reshape.22
  2.3 32.3 %all_gather.6 = bf16[256,128]{1,0:T(8,128)(2,1)S(1)} all-gather(bf16[32,128]{1,0:T(8,128)(2,1)S(1)} %convert_bitcast_fusion.1), channel_id=1, replica_groups=mesh['group'=2,'stn'=8,'chan'=2] {'stn'}, dimensions={0}, use_global_device_ids=true | all-gather | bytes 73728 | tf_op jit(solution)/shard_map/all_gather | solution.py:19
  34.6 0.8 gather_fusion
  35.3 4.2 %fusion.2 = f32[32,1,128,1]{2,1,3,0:T(1,128)S(1)} fusion(bf16[32,5,128,1]{2,3,1,0:T(2,128)(2,1)S(1)} %reshape.45, bf16[1,32,5,128,128]{4,3,2,1,0:T(8,128)(2,1)} %param.4), kind=kOutput, calls=%fused_computation.4 | convolution fusion | flops 5242880 | bytes 5300224 | tf_op jit(solution)/shard_map/nkij,nkj->ni/dot_general | solution.py:21
  39.5 3.4 %psum.43 = f32[4096]{0:T(1024)S(1)} all-reduce(f32[4096]{0:T(1024)S(1)} %bitcast.21), channel_id=1, replica_groups=mesh['group'=2,'stn'=8,'chan'=2] {'chan'}, use_global_device_ids=true, to_apply=%region_2.0 | all-reduce | flops 4096 | bytes 32768 | tf_op jit(solution)/shard_map/psum | solution.py:24
  42.9 0.0 copy-done
  42.9 0.6 multiply_reduce_fusion.2
  43.5 21.9 %all-reduce = (f32[]{:T(128)}, f32[]{:T(128)}) all-reduce(f32[]{:T(128)} %get-tuple-element.3, f32[]{:T(128)} %get-tuple-element.2), channel_id=1, replica_groups=mesh['group'=2,'stn'=8,'chan'=2] {'stn'}, use_global_device_ids=true, to_apply=%region_1.0 | all-reduce | flops 2 | bytes 16 | tf_op jit(solution)/shard_map/psum | solution.py:16
  66.8 0.6 multiply_reduce_fusion.1
  67.4 17.7 %psum.45 = f32[]{:T(128)} all-reduce(f32[]{:T(128)} %multiply_reduce_fusion.1), channel_id=1, replica_groups=mesh['group'=2,'stn'=8,'chan'=2] {'stn'}, use_global_device_ids=true, to_apply=%region_6.0 | all-reduce | flops 1 | bytes 8 | tf_op jit(solution)/shard_map/psum | solution.py:29
  86.5 30.5 %all_gather.7 = bf16[256,128]{1,0:T(8,128)(2,1)S(1)} all-gather(bf16[32,128]{1,0:T(8,128)(2,1)S(1)} %convert_bitcast_fusion), channel_id=1, replica_groups=mesh['group'=2,'stn'=8,'chan'=2] {'stn'}, dimensions={0}, use_global_device_ids=true | all-gather | bytes 73728 | tf_op jit(solution)/shard_map/all_gather | solution.py:19
  117.0 0.8 gather_fusion.1
  117.8 4.2 %fusion = f32[32,1,128,1]{2,1,3,0:T(1,128)S(1)} fusion(bf16[32,5,128,1]{2,3,1,0:T(2,128)(2,1)S(1)} %reshape.47, bf16[1,32,5,128,128]{4,3,2,1,0:T(8,128)(2,1)} %param.4), kind=kOutput, calls=%fused_computation.2 | convolution fusion | flops 5242880 | bytes 5300224 | tf_op jit(solution)/shard_map/nkij,nkj->ni/dot_general | solution.py:21
  122.0 3.4 %psum.46 = f32[4096]{0:T(1024)S(1)} all-reduce(f32[4096]{0:T(1024)S(1)} %bitcast.22), channel_id=1, replica_groups=mesh['group'=2,'stn'=8,'chan'=2] {'chan'}, use_global_device_ids=true, to_apply=%region_7.0 | all-reduce | flops 4096 | bytes 32768 | tf_op jit(solution)/shard_map/psum | solution.py:24
  125.4 0.6 multiply_reduce_fusion
  126.0 19.8 %psum.47 = f32[]{:T(128)} all-reduce(f32[]{:T(128)} %multiply_reduce_fusion), channel_id=1, replica_groups=mesh['group'=2,'stn'=8,'chan'=2] {'stn'}, use_global_device_ids=true, to_apply=%region_9.0 | all-reduce | flops 1 | bytes 8 | tf_op jit(solution)/shard_map/psum | solution.py:25
  147.1 0.6 multiply_subtract_fusion
  (4 shorter events, 0.1 us)
Async XLA Ops:
  0.6 42.3 %copy-start = (f32[4096]{0:T(1024)S(1)}, f32[4096]{0:T(1024)}, u32[]{:S(2)}) copy-start(f32[4096]{0:T(1024)} %param.3) | copy-start | bytes 49156
where the time goes:
time: 148 us
  blocking collectives  129 us (87%)
  matrix products  8.42 us (6%)
  between operations  4.69 us (3%)
  other arithmetic  3.87 us (3%)
  local copies, waits for them, and re-layouts  1.75 us (1%)
    all_gather x2, blocking collectives, local(): whole = lax.all_gather(rounded, 'stn', axis=0, tiled=True)  62.8 us
    psum x1, blocking collectives, local(): norm_now = lax.psum(jnp.sum(residual * residual), 'stn')  21.9 us
    psum x1, blocking collectives, local(): curve = lax.psum(jnp.sum(direction * image), 'stn')  19.8 us
    psum x1, blocking collectives, local(): norm_next = lax.psum(jnp.sum(residual * residual), 'stn')  17.7 us
    dot_general x2, matrix products, local(): jnp.einsum('nkij,nkj->ni', blocks, picked, preferred_element_type=jnp.flo...  8.42 us
    psum x2, blocking collectives, local(): image = lax.psum(partial_value.reshape(-1), 'chan')  6.74 us

commit v1 on v0

v1 whole, which is shorter than its diff:
```python
import functools

import jax
import jax.numpy as jnp
from jax import lax
from jax.experimental import pallas as pl
from jax.experimental.pallas import tpu as pltpu
from jax.sharding import PartitionSpec as P

MESH = pl.DeviceIdType.MESH
ROWS = 16
REACH = 3


def near_offsets(n):
    near = {n // 2}
    for k in range(1, REACH + 1):
        near |= {k % n, (n - k) % n}
    return sorted(near - {0})


def kernel(
    n, chans, pattern, gradient, blocks_hbm, solution, residual,
    blocks, sent0, sent1, whole, picked, mine, theirs, sums0, sums1,
    load_sem, send_sem, recv_sem,
):
    me = lax.axis_index("stn")
    chan = lax.axis_index("chan")
    slot = me * chans + chan
    block_rows, width = gradient.shape
    tiles = blocks.shape[1]
    near = near_offsets(n)
    peers = [(o, c) for o in range(n) for c in range(chans) if (o, c) != (0, 0)]

    load = pltpu.make_async_copy(blocks_hbm.at[0], blocks, load_sem)
    load.start()

    def at(offset, turn):
        return {"stn": lax.rem(me + offset, n), "chan": lax.rem(chan + turn, chans)}

    barrier = pltpu.get_barrier_semaphore()
    for o, c in peers:
        pl.semaphore_signal(barrier, inc=1, device_id=at(o, c), device_id_type=MESH)

    g = gradient[...]
    sent0[me] = g.astype(jnp.bfloat16)
    sums0[slot] = jnp.zeros((8, width), jnp.float32)
    sums1[slot] = jnp.zeros((8, width), jnp.float32)
    pl.semaphore_wait(barrier, len(peers))

    def send(src, dst, which, offset, turn):
        pltpu.make_async_remote_copy(
            src_ref=src, dst_ref=dst, send_sem=send_sem.at[which],
            recv_sem=recv_sem.at[which], device_id=at(offset, turn), device_id_type=MESH,
        ).start()

    def wait(ref, sem):
        pltpu.make_async_copy(ref, ref, sem).wait()

    def apply(sent):
        for o in [0] + near:
            s = lax.rem(me + o, n)
            whole[pl.ds(pl.multiple_of(s * block_rows, block_rows), block_rows), :] = (
                sent[s].astype(jnp.float32)
            )
        for r in range(block_rows):
            for k in range(tiles):
                picked[r : r + 1, k * width : (k + 1) * width] = whole[
                    pl.ds(pattern[k, r], 1), :
                ]
        row = lax.broadcasted_iota(jnp.int32, (ROWS, width), 0)
        out = []
        for base in range(0, block_rows, ROWS):
            left = picked[base : base + ROWS, :].astype(jnp.bfloat16)
            total = jnp.zeros((ROWS, width), jnp.float32)
            for m in range(0, ROWS, 2):
                right = jnp.concatenate(
                    [
                        jnp.concatenate(
                            [blocks[base + m + j, k] for k in range(tiles)], axis=1
                        )
                        for j in range(2)
                    ],
                    axis=0,
                )
                both = lax.dot_general(
                    left, right, (((1,), (1,)), ((), ())),
                    preferred_element_type=jnp.float32,
                )
                total = jnp.where(row == m, both[:, :width], total)
                total = jnp.where(row == m + 1, both[:, width:], total)
            out.append(total)
        return jnp.concatenate(out, axis=0)

    def rowsum(value):
        return jnp.sum(value, axis=0, keepdims=True)

    def total_of(sums):
        return jnp.sum(jnp.sum(sums[...], axis=0), axis=1, keepdims=True)

    for o in near:
        send(sent0.at[me], sent0.at[me], 0, o, 0)
    load.wait()
    wait(sent0.at[pl.ds(0, len(near))], recv_sem.at[0])
    part0 = apply(sent0)

    mine[0] = part0
    send(mine.at[0], theirs.at[0], 1, 0, 1)
    sums0[slot, 0:1, :] = rowsum(g * g)
    sums0[slot, 1:2, :] = rowsum(g * part0)
    for o, c in peers:
        send(sums0.at[slot], sums0.at[slot], 2, o, c)
    wait(theirs.at[0], recv_sem.at[1])
    image = part0 + theirs[0]
    wait(sums0.at[pl.ds(0, len(peers))], recv_sem.at[2])
    totals = total_of(sums0)
    norm0 = totals[0:1, :] * (1.0 / chans)
    curve0 = totals[1:2, :]
    alpha0 = norm0 / curve0
    r1 = g - alpha0 * image

    sent1[me] = r1.astype(jnp.bfloat16)
    for o in near:
        send(sent1.at[me], sent1.at[me], 3, o, 0)
    wait(sent1.at[pl.ds(0, len(near))], recv_sem.at[3])
    part1 = apply(sent1)

    mine[1] = part1
    send(mine.at[1], theirs.at[1], 4, 0, 1)
    sums1[slot, 0:1, :] = rowsum(r1 * r1)
    sums1[slot, 1:2, :] = rowsum(r1 * part1)
    sums1[slot, 2:3, :] = rowsum(r1 * part0 + g * part1)
    for o, c in peers:
        send(sums1.at[slot], sums1.at[slot], 5, o, c)
    wait(theirs.at[1], recv_sem.at[4])
    image1 = part1 + theirs[1]
    wait(sums1.at[pl.ds(0, len(peers))], recv_sem.at[5])
    totals = total_of(sums1)
    norm1 = totals[0:1, :] * (1.0 / chans)
    beta = norm1 / norm0
    curve1 = totals[1:2, :] + beta * (totals[2:3, :] + beta * curve0)
    alpha1 = norm1 / curve1
    solution[...] = alpha0 * g + alpha1 * (r1 + beta * g)
    residual[...] = r1 - alpha1 * (image1 + beta * image)

    wait(sent0.at[pl.ds(0, len(near))], send_sem.at[0])
    wait(theirs.at[0], send_sem.at[1])
    wait(sums0.at[pl.ds(0, len(peers))], send_sem.at[2])
    wait(sent1.at[pl.ds(0, len(near))], send_sem.at[3])
    wait(theirs.at[1], send_sem.at[4])
    wait(sums1.at[pl.ds(0, len(peers))], send_sem.at[5])


def solution(mesh):
    n = mesh.shape["stn"]
    chans = mesh.shape["chan"]

    def local(gradient, normal_blocks, pattern):
        _, block_rows, tiles, width, _ = normal_blocks.shape
        f32, bf16 = jnp.float32, jnp.bfloat16
        vector = jax.ShapeDtypeStruct((block_rows, width), f32)
        vmem = pl.BlockSpec(memory_space=pltpu.VMEM)
        sol, res = pl.pallas_call(
            functools.partial(kernel, n, chans),
            out_shape=(vector, vector),
            in_specs=[
                pl.BlockSpec(memory_space=pltpu.SMEM),
                vmem,
                pl.BlockSpec(memory_space=pl.ANY),
            ],
            out_specs=(vmem, vmem),
            scratch_shapes=[
                pltpu.VMEM((block_rows, tiles, width, width), bf16),
                pltpu.VMEM((n, block_rows, width), bf16),
                pltpu.VMEM((n, block_rows, width), bf16),
                pltpu.VMEM((n * block_rows, width), f32),
                pltpu.VMEM((block_rows, tiles * width), f32),
                pltpu.VMEM((2, block_rows, width), f32),
                pltpu.VMEM((2, block_rows, width), f32),
                pltpu.VMEM((n * chans, 8, width), f32),
                pltpu.VMEM((n * chans, 8, width), f32),
                pltpu.SemaphoreType.DMA,
                pltpu.SemaphoreType.DMA((6,)),
                pltpu.SemaphoreType.DMA((6,)),
            ],
            compiler_params=pltpu.CompilerParams(
                collective_id=0,
                has_side_effects=True,
                vmem_limit_bytes=60 * 1024 * 1024,
            ),
        )(pattern.T, gradient.reshape(block_rows, width), normal_blocks)
        return sol.reshape(-1), res.reshape(-1)

    placed = (
        P(("group", "stn")),
        P("chan", ("group", "stn"), None, None, None),
        P(("group", "stn"), None),
    )
    return jax.shard_map(
        local,
        mesh=mesh,
        in_specs=placed,
        out_specs=(P(("group", "stn")), P(("group", "stn"))),
        check_vma=False,
    )
```

time: 148 us -> 31.3 us (0.21)
  blocking collectives: 129 us -> 0 us
  Pallas kernels: 0 us -> 27.5 us
  matrix products: 8.42 us -> 0 us
  between operations: 4.69 us -> 0.64 us
  other arithmetic: 3.87 us -> 0 us
    psum x5 -> x0, blocking collectives: 66.2 us -> none  [the longest x1 21.9 us: local(): norm_now = lax.psum(jnp.sum(residual * residual), 'stn')]
    all_gather x2 -> x0, blocking collectives: 62.8 us -> none  [local(): whole = lax.all_gather(rounded, 'stn', axis=0, tiled=True)]
    pallas_call x0 -> x1, Pallas kernels: none -> 27.5 us  [local(): pl.pallas_call(functools.partial(kernel, n, chans), out_shape=(vector, ve...]
    dot_general x2 -> x0, matrix products: 8.42 us -> none  [local(): jnp.einsum('nkij,nkj->ni', blocks, picked, preferred_element_type=jnp.flo...]
    unnamed x2, local copies, waits for them, and re-layouts: 0.01 us -> 2.65 us
    reduce_sum x3 -> x0, other arithmetic: 1.82 us -> none  [the longest x2 1.21 us: local(): curve = lax.psum(jnp.sum(direction * image), 'stn')]
    gather x4 -> x0, local copies, waits for them, and re-layouts: 1.55 us -> none  [local(): picked = whole[pattern]]
where the time goes in v1:
time: 31.3 us; the launch traced here: 30.8 us
  Pallas kernels  27.5 us (88%)
  local copies, waits for them, and re-layouts  2.65 us (8%)
  between operations  0.64 us (2%)
    pallas_call x1, Pallas kernels, local(): pl.pallas_call(functools.partial(kernel, n, chans), out_shape=(vector, ve...  27.5 us
    unnamed x2, local copies, waits for them, and re-layouts  2.65 us

profile of v1, /device:TPU:0, one launch (start us, length us, event | category | flops | bytes accessed | tf_op | source)
XLA Modules:
  0.0 30.8 jit_solution(591060180544397601)
XLA Ops:
  0.6 27.5 %shard_map.50 = (f32[32,128]{1,0:T(8,128)}, f32[32,128]{1,0:T(8,128)}) custom-call(s32[5,32]{1,0:T(8,128)} %bitcast.7, f32[32,128]{1,0:T(8,128)} %bitcast.4, bf16[1,32,5,128,128]{4,3,2,1,0:T(8,128)(2,1)} %blocks_hbm.1), custom_call_target="tpu_custom_call" | custom-call | tf_op jit(solution)/shard_map/pallas_call | solution.py:163
  28.1 1.3 %copy.7 = f32[4096]{0:T(1024)} copy(f32[4096]{0:T(1024)} %bitcast.6) | data formatting | bytes 32768
  29.5 1.3 %copy.8 = f32[4096]{0:T(1024)} copy(f32[4096]{0:T(1024)} %bitcast.5) | data formatting | bytes 32768

commit v2 on v1

--- a/solution.py
+++ b/solution.py
@@ -21,7 +21,7 @@
 
 def kernel(
     n, chans, pattern, gradient, blocks_hbm, solution, residual,
-    blocks, sent0, sent1, whole, picked, mine, theirs, sums0, sums1,
+    blocks, high, low, images, whole, picked, mine, theirs, sums,
     load_sem, send_sem, recv_sem,
 ):
     me = lax.axis_index("stn")
@@ -30,6 +30,7 @@
     block_rows, width = gradient.shape
     tiles = blocks.shape[1]
     near = near_offsets(n)
+    far = [o for o in range(1, n) if o not in near]
     peers = [(o, c) for o in range(n) for c in range(chans) if (o, c) != (0, 0)]
 
     load = pltpu.make_async_copy(blocks_hbm.at[0], blocks, load_sem)
@@ -38,15 +39,18 @@
     def at(offset, turn):
         return {"stn": lax.rem(me + offset, n), "chan": lax.rem(chan + turn, chans)}
 
+    greeted = [(o, 0) for o in range(1, n)] + [(0, c) for c in range(1, chans)]
     barrier = pltpu.get_barrier_semaphore()
-    for o, c in peers:
+    for o, c in greeted:
         pl.semaphore_signal(barrier, inc=1, device_id=at(o, c), device_id_type=MESH)
 
     g = gradient[...]
-    sent0[me] = g.astype(jnp.bfloat16)
-    sums0[slot] = jnp.zeros((8, width), jnp.float32)
-    sums1[slot] = jnp.zeros((8, width), jnp.float32)
-    pl.semaphore_wait(barrier, len(peers))
+    rounded = g.astype(jnp.bfloat16)
+    high[me] = rounded
+    low[me] = (g - rounded.astype(jnp.float32)).astype(jnp.bfloat16)
+    images[me, block_rows:, :] = jnp.zeros((8, width), jnp.float32)
+    sums[slot] = jnp.zeros((8, width), jnp.float32)
+    pl.semaphore_wait(barrier, len(greeted))
 
     def send(src, dst, which, offset, turn):
         pltpu.make_async_remote_copy(
@@ -57,11 +61,11 @@
     def wait(ref, sem):
         pltpu.make_async_copy(ref, ref, sem).wait()
 
-    def apply(sent):
+    def apply(vector_of):
         for o in [0] + near:
             s = lax.rem(me + o, n)
             whole[pl.ds(pl.multiple_of(s * block_rows, block_rows), block_rows), :] = (
-                sent[s].astype(jnp.float32)
+                vector_of(s)
             )
         for r in range(block_rows):
             for k in range(tiles):
@@ -95,47 +99,55 @@
     def rowsum(value):
         return jnp.sum(value, axis=0, keepdims=True)
 
-    def total_of(sums):
-        return jnp.sum(jnp.sum(sums[...], axis=0), axis=1, keepdims=True)
-
-    for o in near:
-        send(sent0.at[me], sent0.at[me], 0, o, 0)
+    def total_of(rows):
+        return jnp.sum(jnp.sum(rows, axis=0), axis=1, keepdims=True)
+
+    for o in reversed(near):
+        send(high.at[me], high.at[me], 0, o, 0)
+    for o in reversed(near):
+        send(low.at[me], low.at[me], 1, o, 0)
     load.wait()
-    wait(sent0.at[pl.ds(0, len(near))], recv_sem.at[0])
-    part0 = apply(sent0)
+    wait(high.at[pl.ds(0, len(near))], recv_sem.at[0])
+    part0 = apply(lambda s: high[s].astype(jnp.float32))
 
     mine[0] = part0
-    send(mine.at[0], theirs.at[0], 1, 0, 1)
-    sums0[slot, 0:1, :] = rowsum(g * g)
-    sums0[slot, 1:2, :] = rowsum(g * part0)
-    for o, c in peers:
-        send(sums0.at[slot], sums0.at[slot], 2, o, c)
-    wait(theirs.at[0], recv_sem.at[1])
+    send(mine.at[0], theirs.at[0], 2, 0, 1)
+    images[me, block_rows : block_rows + 1, :] = rowsum(g * g)
+    wait(theirs.at[0], recv_sem.at[2])
     image = part0 + theirs[0]
-    wait(sums0.at[pl.ds(0, len(peers))], recv_sem.at[2])
-    totals = total_of(sums0)
-    norm0 = totals[0:1, :] * (1.0 / chans)
+
+    images[me, :block_rows, :] = image
+    images[me, block_rows + 1 : block_rows + 2, :] = rowsum(g * image)
+    tail = pl.ds(block_rows, 8)
+    for o in reversed(near):
+        send(images.at[me], images.at[me], 3, o, 0)
+    for o in far:
+        send(images.at[me, tail], images.at[me, tail], 4, o, 0)
+    wait(low.at[pl.ds(0, len(near))], recv_sem.at[1])
+    wait(images.at[pl.ds(0, len(near))], recv_sem.at[3])
+    if far:
+        wait(images.at[pl.ds(0, len(far)), tail], recv_sem.at[4])
+    totals = total_of(images[:, block_rows:, :])
+    norm0 = totals[0:1, :]
     curve0 = totals[1:2, :]
     alpha0 = norm0 / curve0
     r1 = g - alpha0 * image
-
-    sent1[me] = r1.astype(jnp.bfloat16)
-    for o in near:
-        send(sent1.at[me], sent1.at[me], 3, o, 0)
-    wait(sent1.at[pl.ds(0, len(near))], recv_sem.at[3])
-    part1 = apply(sent1)
-
+    part1 = apply(
+        lambda s: high[s].astype(jnp.float32)
+        + (low[s].astype(jnp.float32) - alpha0 * images[s, :block_rows, :])
+    )
+
+    sums[slot, 0:1, :] = rowsum(r1 * r1)
+    sums[slot, 1:2, :] = rowsum(r1 * part1)
+    sums[slot, 2:3, :] = rowsum(r1 * part0 + g * part1)
+    for o, c in reversed(peers):
+        send(sums.at[slot], sums.at[slot], 5, o, c)
     mine[1] = part1
-    send(mine.at[1], theirs.at[1], 4, 0, 1)
-    sums1[slot, 0:1, :] = rowsum(r1 * r1)
-    sums1[slot, 1:2, :] = rowsum(r1 * part1)
-    sums1[slot, 2:3, :] = rowsum(r1 * part0 + g * part1)
-    for o, c in peers:
-        send(sums1.at[slot], sums1.at[slot], 5, o, c)
-    wait(theirs.at[1], recv_sem.at[4])
+    send(mine.at[1], theirs.at[1], 6, 0, 1)
+    wait(theirs.at[1], recv_sem.at[6])
     image1 = part1 + theirs[1]
-    wait(sums1.at[pl.ds(0, len(peers))], recv_sem.at[5])
-    totals = total_of(sums1)
+    wait(sums.at[pl.ds(0, len(peers))], recv_sem.at[5])
+    totals = total_of(sums[...])
     norm1 = totals[0:1, :] * (1.0 / chans)
     beta = norm1 / norm0
     curve1 = totals[1:2, :] + beta * (totals[2:3, :] + beta * curve0)
@@ -143,12 +155,14 @@
     solution[...] = alpha0 * g + alpha1 * (r1 + beta * g)
     residual[...] = r1 - alpha1 * (image1 + beta * image)
 
-    wait(sent0.at[pl.ds(0, len(near))], send_sem.at[0])
-    wait(theirs.at[0], send_sem.at[1])
-    wait(sums0.at[pl.ds(0, len(peers))], send_sem.at[2])
-    wait(sent1.at[pl.ds(0, len(near))], send_sem.at[3])
-    wait(theirs.at[1], send_sem.at[4])
-    wait(sums1.at[pl.ds(0, len(peers))], send_sem.at[5])
+    wait(high.at[pl.ds(0, len(near))], send_sem.at[0])
+    wait(low.at[pl.ds(0, len(near))], send_sem.at[1])
+    wait(theirs.at[0], send_sem.at[2])
+    wait(images.at[pl.ds(0, len(near))], send_sem.at[3])
+    if far:
+        wait(images.at[pl.ds(0, len(far)), tail], send_sem.at[4])
+    wait(sums.at[pl.ds(0, len(peers))], send_sem.at[5])
+    wait(theirs.at[1], send_sem.at[6])
 
 
 def solution(mesh):
@@ -173,15 +187,15 @@
                 pltpu.VMEM((block_rows, tiles, width, width), bf16),
                 pltpu.VMEM((n, block_rows, width), bf16),
                 pltpu.VMEM((n, block_rows, width), bf16),
+                pltpu.VMEM((n, block_rows + 8, width), f32),
                 pltpu.VMEM((n * block_rows, width), f32),
                 pltpu.VMEM((block_rows, tiles * width), f32),
                 pltpu.VMEM((2, block_rows, width), f32),
                 pltpu.VMEM((2, block_rows, width), f32),
                 pltpu.VMEM((n * chans, 8, width), f32),
-                pltpu.VMEM((n * chans, 8, width), f32),
                 pltpu.SemaphoreType.DMA,
-                pltpu.SemaphoreType.DMA((6,)),
-                pltpu.SemaphoreType.DMA((6,)),
+                pltpu.SemaphoreType.DMA((7,)),
+                pltpu.SemaphoreType.DMA((7,)),
             ],
             compiler_params=pltpu.CompilerParams(
                 collective_id=0,

time: 31.3 us -> 28 us (0.89)
  Pallas kernels: 27.5 us -> 24.2 us
    pallas_call x1, Pallas kernels: 27.5 us -> 24.2 us  [local(): pl.pallas_call(functools.partial(kernel, n, chans), out_shape=(vector, ve...]
where the time goes in v2:
time: 28 us; the launch traced here: 27.5 us
  Pallas kernels  24.2 us (86%)
  local copies, waits for them, and re-layouts  2.65 us (9%)
  between operations  0.64 us (2%)
    pallas_call x1, Pallas kernels, local(): pl.pallas_call(functools.partial(kernel, n, chans), out_shape=(vector, ve...  24.2 us
    unnamed x2, local copies, waits for them, and re-layouts  2.65 us

profile of v2, /device:TPU:0, one launch (start us, length us, event | category | flops | bytes accessed | tf_op | source)
XLA Modules:
  0.0 27.5 jit_solution(16167981042621485849)
XLA Ops:
  0.6 24.2 %shard_map.50 = (f32[32,128]{1,0:T(8,128)}, f32[32,128]{1,0:T(8,128)}) custom-call(s32[5,32]{1,0:T(8,128)} %bitcast.7, f32[32,128]{1,0:T(8,128)} %bitcast.4, bf16[1,32,5,128,128]{4,3,2,1,0:T(8,128)(2,1)} %blocks_hbm.1), custom_call_target="tpu_custom_call" | custom-call | tf_op jit(solution)/shard_map/pallas_call | solution.py:177
  24.9 1.3 %copy.7 = f32[4096]{0:T(1024)} copy(f32[4096]{0:T(1024)} %bitcast.6) | data formatting | bytes 32768
  26.2 1.3 %copy.8 = f32[4096]{0:T(1024)} copy(f32[4096]{0:T(1024)} %bitcast.5) | data formatting | bytes 32768

commit v3 on v2

--- a/solution.py
+++ b/solution.py
@@ -20,8 +20,9 @@
 
 
 def kernel(
-    n, chans, pattern, gradient, blocks_hbm, solution, residual,
-    blocks, high, low, images, whole, picked, mine, theirs, sums,
+    n, chans, pattern_hbm, gradient_hbm, blocks_hbm,
+    start_out, step_out, direction_out, before_out, image_out,
+       pattern, gradient, blocks, high, low, images, whole, picked, mine, theirs, sums,
     load_sem, send_sem, recv_sem,
 ):
     me = lax.axis_index("stn")
@@ -33,9 +34,6 @@
     far = [o for o in range(1, n) if o not in near]
     peers = [(o, c) for o in range(n) for c in range(chans) if (o, c) != (0, 0)]
 
-    load = pltpu.make_async_copy(blocks_hbm.at[0], blocks, load_sem)
-    load.start()
-
     def at(offset, turn):
         return {"stn": lax.rem(me + offset, n), "chan": lax.rem(chan + turn, chans)}
 
@@ -44,6 +42,13 @@
     for o, c in greeted:
         pl.semaphore_signal(barrier, inc=1, device_id=at(o, c), device_id_type=MESH)
 
+    begin = pltpu.make_async_copy(gradient_hbm, gradient, load_sem.at[0])
+    begin.start()
+    fetch = pltpu.make_async_copy(pattern_hbm, pattern, load_sem.at[1])
+    fetch.start()
+    load = pltpu.make_async_copy(blocks_hbm.at[0], blocks, load_sem.at[2])
+    load.start()
+    begin.wait()
     g = gradient[...]
     rounded = g.astype(jnp.bfloat16)
     high[me] = rounded
@@ -106,6 +111,7 @@
         send(high.at[me], high.at[me], 0, o, 0)
     for o in reversed(near):
         send(low.at[me], low.at[me], 1, o, 0)
+    fetch.wait()
     load.wait()
     wait(high.at[pl.ds(0, len(near))], recv_sem.at[0])
     part0 = apply(lambda s: high[s].astype(jnp.float32))
@@ -152,8 +158,11 @@
     beta = norm1 / norm0
     curve1 = totals[1:2, :] + beta * (totals[2:3, :] + beta * curve0)
     alpha1 = norm1 / curve1
-    solution[...] = alpha0 * g + alpha1 * (r1 + beta * g)
-    residual[...] = r1 - alpha1 * (image1 + beta * image)
+    step_out[...] = jnp.broadcast_to(alpha1, (block_rows, width))
+    start_out[...] = alpha0 * g
+    direction_out[...] = r1 + beta * g
+    before_out[...] = r1
+    image_out[...] = image1 + beta * image
 
     wait(high.at[pl.ds(0, len(near))], send_sem.at[0])
     wait(low.at[pl.ds(0, len(near))], send_sem.at[1])
@@ -174,16 +183,14 @@
         f32, bf16 = jnp.float32, jnp.bfloat16
         vector = jax.ShapeDtypeStruct((block_rows, width), f32)
         vmem = pl.BlockSpec(memory_space=pltpu.VMEM)
-        sol, res = pl.pallas_call(
+        start, alpha, direction, before, image = pl.pallas_call(
             functools.partial(kernel, n, chans),
-            out_shape=(vector, vector),
-            in_specs=[
-                pl.BlockSpec(memory_space=pltpu.SMEM),
-                vmem,
-                pl.BlockSpec(memory_space=pl.ANY),
-            ],
-            out_specs=(vmem, vmem),
+            out_shape=(vector,) * 5,
+            in_specs=[pl.BlockSpec(memory_space=pl.ANY)] * 3,
+            out_specs=(vmem,) * 5,
             scratch_shapes=[
+                pltpu.SMEM((tiles, block_rows), jnp.int32),
+                pltpu.VMEM((block_rows, width), f32),
                 pltpu.VMEM((block_rows, tiles, width, width), bf16),
                 pltpu.VMEM((n, block_rows, width), bf16),
                 pltpu.VMEM((n, block_rows, width), bf16),
@@ -193,7 +200,7 @@
                 pltpu.VMEM((2, block_rows, width), f32),
                 pltpu.VMEM((2, block_rows, width), f32),
                 pltpu.VMEM((n * chans, 8, width), f32),
-                pltpu.SemaphoreType.DMA,
+                pltpu.SemaphoreType.DMA((3,)),
                 pltpu.SemaphoreType.DMA((7,)),
                 pltpu.SemaphoreType.DMA((7,)),
             ],
@@ -203,7 +210,9 @@
                 vmem_limit_bytes=60 * 1024 * 1024,
             ),
         )(pattern.T, gradient.reshape(block_rows, width), normal_blocks)
-        return sol.reshape(-1), res.reshape(-1)
+        solution = start + alpha * direction
+        residual = before - alpha * image
+        return solution.reshape(-1), residual.reshape(-1)
 
     placed = (
         P(("group", "stn")),

time: 28 us -> 25.9 us (0.925)
  local copies, waits for them, and re-layouts: 2.65 us -> 0 us
  other arithmetic: 0 us -> 1.41 us
  Pallas kernels: 24.2 us -> 23.6 us
    unnamed x2 -> x0, local copies, waits for them, and re-layouts: 2.65 us -> none
    reshape x0 -> x1, other arithmetic: none -> 1.41 us  [local(): return (solution.reshape(-1), residual.reshape(-1))]
    pallas_call x1, Pallas kernels: 24.2 us -> 23.6 us  [local(): pl.pallas_call(functools.partial(kernel, n, chans), out_shape=(vector,) *...]
where the time goes in v3:
time: 25.9 us; the launch traced here: 25.6 us
  Pallas kernels  23.6 us (91%)
  other arithmetic  1.41 us (5%)
  between operations  0.64 us (2%)
    pallas_call x1, Pallas kernels, local(): pl.pallas_call(functools.partial(kernel, n, chans), out_shape=(vector,) *...  23.6 us
    reshape x1, other arithmetic, local(): return (solution.reshape(-1), residual.reshape(-1))  1.41 us

profile of v3, /device:TPU:0, one launch (start us, length us, event | category | flops | bytes accessed | tf_op | source)
XLA Modules:
  0.0 25.6 jit_solution(12939390841301947331)
XLA Ops:
  0.6 23.6 %shard_map.50 = (f32[32,128]{1,0:T(8,128)}, f32[32,128]{1,0:T(8,128)}, f32[32,128]{1,0:T(8,128)}, f32[32,128]{1,0:T(8,128)}, f32[32,128]{1,0:T(8,128)}) custom-call(s32[5,32]{1,0:T(8,128)} %bitcast.7, f32[32,128]{1,0:T(8,128)} %bitcast.6, bf16[1,32,5,128,128]{4,3,2,1,0:T(8,128)(2,1)} %blocks_hbm.1), custom_call_target="tpu_custom_call" | custom-call | tf_op jit(solution)/shard_map/pallas_call | solution.py:186
  24.2 1.4 %subtract_bitcast_fusion = (f32[4096]{0:T(1024)}, f32[4096]{0:T(1024)}) fusion(f32[32,128]{1,0:T(8,128)} %get-tuple-element.10, f32[32,128]{1,0:T(8,128)} %get-tuple-element.8, f32[32,128]{1,0:T(8,128)} %get-tuple-element.11, f32[32,128]{1,0:T(8,128)} %get-tuple-element.7, f32[32,128]{1,0:T(8,128)} %get-tuple-element.9), kind=kLoop, calls=%fused_computation | loop fusion | flops 16384 | bytes 114688 | tf_op jit(solution)/shard_map/reshape | solution.py:215

commit v4 on v3

--- a/solution.py
+++ b/solution.py
@@ -31,6 +31,10 @@
     block_rows, width = gradient.shape
     tiles = blocks.shape[1]
     near = near_offsets(n)
+    half = n // 2
+    others = [o for o in near if o != half]
+    early = [0, 3]
+    late = [k for k in range(tiles) if k not in early]
     far = [o for o in range(1, n) if o not in near]
     peers = [(o, c) for o in range(n) for c in range(chans) if (o, c) != (0, 0)]
 
@@ -66,28 +70,34 @@
     def wait(ref, sem):
         pltpu.make_async_copy(ref, ref, sem).wait()
 
-    def apply(vector_of):
-        for o in [0] + near:
+    def gather(vector_of, offsets, group):
+        for o in offsets:
             s = lax.rem(me + o, n)
             whole[pl.ds(pl.multiple_of(s * block_rows, block_rows), block_rows), :] = (
                 vector_of(s)
             )
         for r in range(block_rows):
-            for k in range(tiles):
+            for k in group:
                 picked[r : r + 1, k * width : (k + 1) * width] = whole[
                     pl.ds(pattern[k, r], 1), :
                 ]
+
+    def multiply(group):
         row = lax.broadcasted_iota(jnp.int32, (ROWS, width), 0)
         out = []
         for base in range(0, block_rows, ROWS):
-            left = picked[base : base + ROWS, :].astype(jnp.bfloat16)
+            left = jnp.concatenate(
+                [
+                    picked[base : base + ROWS, k * width : (k + 1) * width]
+                    for k in group
+                ],
+                axis=1,
+            ).astype(jnp.bfloat16)
             total = jnp.zeros((ROWS, width), jnp.float32)
             for m in range(0, ROWS, 2):
                 right = jnp.concatenate(
                     [
-                        jnp.concatenate(
-                            [blocks[base + m + j, k] for k in range(tiles)], axis=1
-                        )
+                        jnp.concatenate([blocks[base + m + j, k] for k in group], axis=1)
                         for j in range(2)
                     ],
                     axis=0,
@@ -107,14 +117,22 @@
     def total_of(rows):
         return jnp.sum(jnp.sum(rows, axis=0), axis=1, keepdims=True)
 
-    for o in reversed(near):
+    def first(s):
+        return high[s].astype(jnp.float32)
+
+    for o in others[::-1]:
         send(high.at[me], high.at[me], 0, o, 0)
+    send(high.at[me], high.at[me], 7, half, 0)
     for o in reversed(near):
         send(low.at[me], low.at[me], 1, o, 0)
     fetch.wait()
     load.wait()
-    wait(high.at[pl.ds(0, len(near))], recv_sem.at[0])
-    part0 = apply(lambda s: high[s].astype(jnp.float32))
+    wait(high.at[0], recv_sem.at[7])
+    gather(first, [0, half], early)
+    part0 = multiply(early)
+    wait(high.at[pl.ds(0, len(others))], recv_sem.at[0])
+    gather(first, others, late)
+    part0 = part0 + multiply(late)
 
     mine[0] = part0
     send(mine.at[0], theirs.at[0], 2, 0, 1)
@@ -138,21 +156,24 @@
     curve0 = totals[1:2, :]
     alpha0 = norm0 / curve0
     r1 = g - alpha0 * image
-    part1 = apply(
+    gather(
         lambda s: high[s].astype(jnp.float32)
-        + (low[s].astype(jnp.float32) - alpha0 * images[s, :block_rows, :])
+        + (low[s].astype(jnp.float32) - alpha0 * images[s, :block_rows, :]),
+        [0] + near,
+        range(tiles),
     )
+    part1 = multiply(range(tiles))
 
     sums[slot, 0:1, :] = rowsum(r1 * r1)
     sums[slot, 1:2, :] = rowsum(r1 * part1)
     sums[slot, 2:3, :] = rowsum(r1 * part0 + g * part1)
     for o, c in reversed(peers):
-        send(sums.at[slot], sums.at[slot], 5, o, c)
+        send(sums.at[slot, pl.ds(0, 4)], sums.at[slot, pl.ds(0, 4)], 5, o, c)
     mine[1] = part1
     send(mine.at[1], theirs.at[1], 6, 0, 1)
     wait(theirs.at[1], recv_sem.at[6])
     image1 = part1 + theirs[1]
-    wait(sums.at[pl.ds(0, len(peers))], recv_sem.at[5])
+    wait(sums.at[pl.ds(0, len(peers)), pl.ds(0, 4)], recv_sem.at[5])
     totals = total_of(sums[...])
     norm1 = totals[0:1, :] * (1.0 / chans)
     beta = norm1 / norm0
@@ -164,13 +185,14 @@
     before_out[...] = r1
     image_out[...] = image1 + beta * image
 
-    wait(high.at[pl.ds(0, len(near))], send_sem.at[0])
+    wait(high.at[pl.ds(0, len(others))], send_sem.at[0])
+    wait(high.at[0], send_sem.at[7])
     wait(low.at[pl.ds(0, len(near))], send_sem.at[1])
     wait(theirs.at[0], send_sem.at[2])
     wait(images.at[pl.ds(0, len(near))], send_sem.at[3])
     if far:
         wait(images.at[pl.ds(0, len(far)), tail], send_sem.at[4])
-    wait(sums.at[pl.ds(0, len(peers))], send_sem.at[5])
+    wait(sums.at[pl.ds(0, len(peers)), pl.ds(0, 4)], send_sem.at[5])
     wait(theirs.at[1], send_sem.at[6])
 
 
@@ -181,7 +203,7 @@
     def local(gradient, normal_blocks, pattern):
         _, block_rows, tiles, width, _ = normal_blocks.shape
         f32, bf16 = jnp.float32, jnp.bfloat16
-        vector = jax.ShapeDtypeStruct((block_rows, width), f32)
+        vector = pltpu.VMEM((block_rows, width), f32)
         vmem = pl.BlockSpec(memory_space=pltpu.VMEM)
         start, alpha, direction, before, image = pl.pallas_call(
             functools.partial(kernel, n, chans),
@@ -201,8 +223,8 @@
                 pltpu.VMEM((2, block_rows, width), f32),
                 pltpu.VMEM((n * chans, 8, width), f32),
                 pltpu.SemaphoreType.DMA((3,)),
-                pltpu.SemaphoreType.DMA((7,)),
-                pltpu.SemaphoreType.DMA((7,)),
+                pltpu.SemaphoreType.DMA((8,)),
+                pltpu.SemaphoreType.DMA((8,)),
             ],
             compiler_params=pltpu.CompilerParams(
                 collective_id=0,

time: 25.9 us -> 23.3 us (0.90)
  Pallas kernels: 23.6 us -> 21.8 us
  other arithmetic: 1.41 us -> 0.62 us
    pallas_call x1, Pallas kernels: 23.6 us -> 21.8 us  [local(): pl.pallas_call(functools.partial(kernel, n, chans), out_shape=(vector,) *...]
    reshape x1, other arithmetic: 1.41 us -> 0.62 us  [local(): return (solution.reshape(-1), residual.reshape(-1))]
where the time goes in v4:
time: 23.3 us; the launch traced here: 23.1 us
  Pallas kernels  21.8 us (94%)
  between operations  0.64 us (3%)
  other arithmetic  0.62 us (3%)
    pallas_call x1, Pallas kernels, local(): pl.pallas_call(functools.partial(kernel, n, chans), out_shape=(vector,) *...  21.8 us
    reshape x1, other arithmetic, local(): return (solution.reshape(-1), residual.reshape(-1))  0.62 us

profile of v4, /device:TPU:0, one launch (start us, length us, event | category | flops | bytes accessed | tf_op | source)
XLA Modules:
  0.0 23.1 jit_solution(12413259620395127018)
XLA Ops:
  0.6 21.8 %shard_map.50 = (f32[32,128]{1,0:T(8,128)S(1)}, f32[32,128]{1,0:T(8,128)S(1)}, f32[32,128]{1,0:T(8,128)S(1)}, f32[32,128]{1,0:T(8,128)S(1)}, f32[32,128]{1,0:T(8,128)S(1)}) custom-call(s32[5,32]{1,0:T(8,128)} %bitcast.7, f32[32,128]{1,0:T(8,128)} %bitcast.6, bf16[1,32,5,128,128]{4,3,2,1,0:T(8,128)(2,1)} %blocks_hbm.1), custom_call_target="tpu_custom_call" | custom-call | tf_op jit(solution)/shard_map/pallas_call | solution.py:208
  22.5 0.6 %subtract_bitcast_fusion = (f32[4096]{0:T(1024)}, f32[4096]{0:T(1024)}) fusion(f32[32,128]{1,0:T(8,128)S(1)} %get-tuple-element.10, f32[32,128]{1,0:T(8,128)S(1)} %get-tuple-element.8, f32[32,128]{1,0:T(8,128)S(1)} %get-tuple-element.11, f32[32,128]{1,0:T(8,128)S(1)} %get-tuple-element.7, f32[32,128]{1,0:T(8,128)S(1)} %get-tuple-element.9), kind=kLoop, calls=%fused_computation | loop fusion | flops 16384 | bytes 114688 | tf_op jit(solution)/shard_map/reshape | solution.py:237

commit v5 on v4

--- a/solution.py
+++ b/solution.py
@@ -142,16 +142,17 @@
 
     images[me, :block_rows, :] = image
     images[me, block_rows + 1 : block_rows + 2, :] = rowsum(g * image)
-    tail = pl.ds(block_rows, 8)
+    tail = pl.ds(block_rows, 4)
+    used = pl.ds(0, block_rows + 4)
     for o in reversed(near):
-        send(images.at[me], images.at[me], 3, o, 0)
+        send(images.at[me, used], images.at[me, used], 3, o, 0)
     for o in far:
         send(images.at[me, tail], images.at[me, tail], 4, o, 0)
     wait(low.at[pl.ds(0, len(near))], recv_sem.at[1])
-    wait(images.at[pl.ds(0, len(near))], recv_sem.at[3])
+    wait(images.at[pl.ds(0, len(near)), used], recv_sem.at[3])
     if far:
         wait(images.at[pl.ds(0, len(far)), tail], recv_sem.at[4])
-    totals = total_of(images[:, block_rows:, :])
+    totals = total_of(images[:, block_rows : block_rows + 4, :])
     norm0 = totals[0:1, :]
     curve0 = totals[1:2, :]
     alpha0 = norm0 / curve0
@@ -189,7 +190,7 @@
     wait(high.at[0], send_sem.at[7])
     wait(low.at[pl.ds(0, len(near))], send_sem.at[1])
     wait(theirs.at[0], send_sem.at[2])
-    wait(images.at[pl.ds(0, len(near))], send_sem.at[3])
+    wait(images.at[pl.ds(0, len(near)), used], send_sem.at[3])
     if far:
         wait(images.at[pl.ds(0, len(far)), tail], send_sem.at[4])
     wait(sums.at[pl.ds(0, len(peers)), pl.ds(0, 4)], send_sem.at[5])

time: 23.3 us -> 23 us (0.987)
  Pallas kernels: 21.8 us -> 21.5 us
    pallas_call x1, Pallas kernels: 21.8 us -> 21.5 us  [local(): pl.pallas_call(functools.partial(kernel, n, chans), out_shape=(vector,) *...]
where the time goes in v5:
time: 23 us; the launch traced here: 22.7 us
  Pallas kernels  21.5 us (93%)
  between operations  0.64 us (3%)
  other arithmetic  0.62 us (3%)
    pallas_call x1, Pallas kernels, local(): pl.pallas_call(functools.partial(kernel, n, chans), out_shape=(vector,) *...  21.5 us
    reshape x1, other arithmetic, local(): return (solution.reshape(-1), residual.reshape(-1))  0.62 us

profile of v5, /device:TPU:0, one launch (start us, length us, event | category | flops | bytes accessed | tf_op | source)
XLA Modules:
  0.0 22.7 jit_solution(8346543877236780961)
XLA Ops:
  0.6 21.5 %shard_map.50 = (f32[32,128]{1,0:T(8,128)S(1)}, f32[32,128]{1,0:T(8,128)S(1)}, f32[32,128]{1,0:T(8,128)S(1)}, f32[32,128]{1,0:T(8,128)S(1)}, f32[32,128]{1,0:T(8,128)S(1)}) custom-call(s32[5,32]{1,0:T(8,128)} %bitcast.7, f32[32,128]{1,0:T(8,128)} %bitcast.6, bf16[1,32,5,128,128]{4,3,2,1,0:T(8,128)(2,1)} %blocks_hbm.1), custom_call_target="tpu_custom_call" | custom-call | tf_op jit(solution)/shard_map/pallas_call | solution.py:209
  22.1 0.6 %subtract_bitcast_fusion = (f32[4096]{0:T(1024)}, f32[4096]{0:T(1024)}) fusion(f32[32,128]{1,0:T(8,128)S(1)} %get-tuple-element.10, f32[32,128]{1,0:T(8,128)S(1)} %get-tuple-element.8, f32[32,128]{1,0:T(8,128)S(1)} %get-tuple-element.11, f32[32,128]{1,0:T(8,128)S(1)} %get-tuple-element.7, f32[32,128]{1,0:T(8,128)S(1)} %get-tuple-element.9), kind=kLoop, calls=%fused_computation | loop fusion | flops 16384 | bytes 114688 | tf_op jit(solution)/shard_map/reshape | solution.py:238
